TPU v7x, 256 devices: a whole 4x4x8 slice. The times are simulated.
256 devices in a mesh: row: 8 (over z_lo, core), col: 32 (over y, x, z_hi).
Axes of the slice: x: 4, y: 4, z: 8 (z_hi: 2, z_lo: 4; z = z_hi * 4 + z_lo), core: 2. Of those that a mesh axis runs over, the one named last changes fastest.
Arguments:
- query_vecs: bfloat16 [16384, 1280], P(('row', 'col')), may hold values from -6 to 6
- key_vecs: bfloat16 [16384, 1280], P(('col', 'row')), may hold values from -6 to 6
- value_vecs: bfloat16 [16384, 1280], P(('col', 'row')), may hold values from -6 to 6
- attn_out: bfloat16 [16384, 1280], P(('row', 'col')), may hold values from -6 to 6
- out_grad: bfloat16 [16384, 1280], P(('row', 'col')), may hold values from -180 to 180
- saved_lse: float32 [16384, 16], P(('row', 'col')), may hold values from 9 to 10.5
- kept_mask: int32 [16384], P(('col', 'row')), may hold values from 0 to 1, as said below
Outputs:
- query_grad: bfloat16 [16384, 1280], P(('row', 'col'))
- key_grad: bfloat16 [16384, 1280], P(('col', 'row'))
- value_grad: bfloat16 [16384, 1280], P(('col', 'row'))
Inputs may be any that keep to these rules, and one draw needn't show every extreme that they name: `kept_mask`: 1 marks a kept token, 0 a token dropped from the scene.
All inputs are finite; a program needn't handle non-finite values.
Results may differ from a plain program's by a relative error of at most 0.0049.
Values may be sent and summed in bfloat16 or wider, within the bound.
A program may use at most 128 MiB of HBM per device.

v0:
```python
import jax
import jax.numpy as jnp
from jax import lax
from jax.sharding import PartitionSpec as P


def attend(query_blk, grad_blk, lse_blk, delta_blk, key_blk, value_blk, keep_blk, heads, head_dim):
    scaling = head_dim ** (-0.5)
    query_count = query_blk.shape[0]
    key_count = key_blk.shape[0]
    width = heads * head_dim
    keep_row = keep_blk.astype(jnp.float32)[None, :]

    def one_head(head_index, carry):
        query_acc, key_acc, value_acc = carry
        column = head_index * head_dim
        query_h = lax.dynamic_slice_in_dim(query_blk, column, head_dim, 1)
        grad_h = lax.dynamic_slice_in_dim(grad_blk, column, head_dim, 1)
        key_h = lax.dynamic_slice_in_dim(key_blk, column, head_dim, 1)
        value_h = lax.dynamic_slice_in_dim(value_blk, column, head_dim, 1)
        lse_h = lax.dynamic_slice_in_dim(lse_blk, head_index, 1, 1)
        delta_h = lax.dynamic_slice_in_dim(delta_blk, head_index, 1, 1)
        scores = (
            jnp.einsum("qd,kd->qk", query_h, key_h, preferred_element_type=jnp.float32) * scaling
        )
        probs = keep_row * jnp.exp(scores - lse_h)
        probs_low = probs.astype(jnp.bfloat16)
        value_part = jnp.einsum("qk,qd->kd", probs_low, grad_h, preferred_element_type=jnp.float32)
        grad_probs = jnp.einsum("qd,kd->qk", grad_h, value_h, preferred_element_type=jnp.float32)
        grad_scores = (probs * (grad_probs - delta_h)).astype(jnp.bfloat16)
        query_part = jnp.dot(grad_scores, key_h, preferred_element_type=jnp.float32)
        key_part = jnp.einsum("qk,qd->kd", grad_scores, query_h, preferred_element_type=jnp.float32)
        query_acc = lax.dynamic_update_slice_in_dim(query_acc, query_part, column, 1)
        key_acc = lax.dynamic_update_slice_in_dim(key_acc, key_part, column, 1)
        value_acc = lax.dynamic_update_slice_in_dim(value_acc, value_part, column, 1)
        return (query_acc, key_acc, value_acc)

    start = (
        jnp.zeros((query_count, width), jnp.float32),
        jnp.zeros((key_count, width), jnp.float32),
        jnp.zeros((key_count, width), jnp.float32),
    )
    return lax.fori_loop(0, heads, one_head, start)


def on_device(query_vecs, key_vecs, value_vecs, attn_out, out_grad, saved_lse, kept_mask):
    local_rows, width = query_vecs.shape
    heads = saved_lse.shape[1]
    head_dim = width // heads
    scaling = head_dim ** (-0.5)
    products = out_grad.astype(jnp.float32) * attn_out.astype(jnp.float32)
    delta = jnp.sum(products.reshape(local_rows, heads, head_dim), axis=2)
    keep_low = kept_mask.astype(jnp.bfloat16)
    query_blk, grad_blk = (
        lax.all_gather(query_vecs, "col", axis=0, tiled=True),
        lax.all_gather(out_grad, "col", axis=0, tiled=True),
    )
    lse_blk, delta_blk = (
        lax.all_gather(saved_lse, "col", axis=0, tiled=True),
        lax.all_gather(delta, "col", axis=0, tiled=True),
    )
    key_blk, value_blk, keep_blk = (
        lax.all_gather(key_vecs, "row", axis=0, tiled=True),
        lax.all_gather(value_vecs, "row", axis=0, tiled=True),
        lax.all_gather(keep_low, "row", axis=0, tiled=True),
    )
    query_acc, key_acc, value_acc = attend(
        query_blk, grad_blk, lse_blk, delta_blk, key_blk, value_blk, keep_blk, heads, head_dim
    )
    query_sum = lax.psum_scatter(query_acc, "col", scatter_dimension=0, tiled=True)
    key_sum, value_sum = (
        lax.psum_scatter(key_acc, "row", scatter_dimension=0, tiled=True),
        lax.psum_scatter(value_acc, "row", scatter_dimension=0, tiled=True),
    )
    query_grad = (query_sum * scaling).astype(jnp.bfloat16)
    key_grad = (key_sum * scaling).astype(jnp.bfloat16)
    value_grad = value_sum.astype(jnp.bfloat16)
    return (query_grad, key_grad, value_grad)


def solution(mesh):
    return jax.shard_map(
        on_device,
        mesh=mesh,
        in_specs=(
            P(("row", "col"), None),
            P(("col", "row"), None),
            P(("col", "row"), None),
            P(("row", "col"), None),
            P(("row", "col"), None),
            P(("row", "col"), None),
            P(("col", "row")),
        ),
        out_specs=(P(("row", "col"), None), P(("col", "row"), None), P(("col", "row"), None)),
        check_vma=False,
    )
```

profile of v0, /device:TPU:1, one launch (start us, length us, event | category | flops | bytes accessed | tf_op | source)
XLA Modules:
  0.0 1089.5 jit_solution(15216724498841455936)
XLA Ops:
  12.8 16.3 %all-reduce = bf16[512]{0:T(512)(128)(2,1)S(1)} all-reduce(bf16[512]{0:T(512)(128)(2,1)S(1)} %dynamic-update-slice), channel_id=1, replica_groups=mesh['row'=8,'col'=32] {'row'}, use_global_device_ids=true, to_apply=%add | all-reduce | flops 512 | bytes 2048
  29.1 106.7 %all-gather = f32[32,64,16]{1,2,0:T(8,128)S(1)} all-gather(f32[1,64,16]{1,2,0:T(8,128)} %bitcast.28), channel_id=1, replica_groups=mesh['row'=8,'col'=32] {'col'}, dimensions={0}, use_global_device_ids=true | all-gather | bytes 135168 | tf_op jit(solution)/shard_map/all_gather | solution.py:59
  137.7 107.0 %all-gather.1 = f32[32,64,16]{1,2,0:T(8,128)S(1)} all-gather(f32[1,64,16]{1,2,0:T(8,128)S(1)} %copy.19), channel_id=1, replica_groups=mesh['row'=8,'col'=32] {'col'}, dimensions={0}, use_global_device_ids=true | all-gather | bytes 135168 | tf_op jit(solution)/shard_map/all_gather | solution.py:60
  244.9 94.0 %all-gather.11.cloned.1.call-done = bf16[2048,1280]{1,0:T(8,128)(2,1)} async-done(((bf16[64,1280]{1,0:T(8,128)(2,1)}), bf16[2048,1280]{1,0:T(8,128)(2,1)}) %all-gather.11.cloned.1.call-update) | async-done | bytes 5242896 | tf_op jit(solution)/shard_map/all_gather | solution.py:56
  341.2 5.1 broadcast_in_dim.9
  346.3 185.1 %while.17 = (s32[]{:T(128)}, f32[2048,1280]{0,1:T(8,128)}, f32[512,1280]{0,1:T(8,128)}, f32[512,1280]{0,1:T(8,128)S(1)}, f32[1,512]{1,0:T(1,128)S(1)}, /*index=5...) while((s32[]{:T(128)}, f32[2048,1280]{0,1:T(8,128)}, ...), condition=%wide.region_2.0_spmd, body=%wide.region_1.0_spmd.sunk | while | flops 846200832 | bytes 22404296 | solution.py:43
  355.3 2.6 convolution_dynamic-update-slice_fusion.4
  364.3 2.6 convolution_dynamic-update-slice_fusion.5
  366.9 2.6 convolution_dynamic-update-slice_fusion.4
  375.9 2.6 convolution_dynamic-update-slice_fusion.5
  378.5 2.6 convolution_dynamic-update-slice_fusion.4
  390.1 2.7 convolution_dynamic-update-slice_fusion.4
  401.8 2.6 convolution_dynamic-update-slice_fusion.4
  413.4 2.6 convolution_dynamic-update-slice_fusion.4
  425.0 2.7 convolution_dynamic-update-slice_fusion.4
  436.6 2.6 convolution_dynamic-update-slice_fusion.4
  445.7 2.6 convolution_dynamic-update-slice_fusion.5
  448.3 2.7 convolution_dynamic-update-slice_fusion.4
  459.9 2.6 convolution_dynamic-update-slice_fusion.4
  469.0 2.6 convolution_dynamic-update-slice_fusion.5
  471.6 2.6 convolution_dynamic-update-slice_fusion.4
  483.2 2.7 convolution_dynamic-update-slice_fusion.4
  492.2 2.6 convolution_dynamic-update-slice_fusion.5
  494.8 2.6 convolution_dynamic-update-slice_fusion.4
  503.9 2.6 convolution_dynamic-update-slice_fusion.5
  506.4 2.6 convolution_dynamic-update-slice_fusion.4
  515.5 2.6 convolution_dynamic-update-slice_fusion.5
  518.1 2.6 convolution_dynamic-update-slice_fusion.4
  537.6 11.3 %copy.21 = f32[2048,1280]{1,0:T(8,128)} copy(f32[2048,1280]{0,1:T(8,128)} %get-tuple-element.189) | data formatting | bytes 20971520 | tf_op jit(solution)/shard_map/while | solution.py:43
  549.0 20.1 %reduce-scatter.8.cloned.1.call-done = f32[64,1280]{1,0:T(8,128)} async-done(((f32[512,1280]{1,0:T(8,128)}), f32[64,1280]{1,0:T(8,128)}) %reduce-scatter.8.cloned.1.call-update) | async-done | bytes 327696 | tf_op jit(solution)/shard_map/reduce_scatter | solution.py:73
  570.7 43.1 %reduce-scatter.6.cloned.1.call-done = f32[64,1280]{1,0:T(8,128)} async-done(((f32[512,1280]{1,0:T(8,128)}), f32[64,1280]{1,0:T(8,128)}) %reduce-scatter.6.cloned.1.call-update) | async-done | bytes 327696 | tf_op jit(solution)/shard_map/reduce_scatter | solution.py:72
  615.4 465.6 %reduce-scatter.4.cloned.1.call-done = f32[64,1280]{1,0:T(8,128)} async-done(((f32[2048,1280]{1,0:T(8,128)}), f32[64,1280]{1,0:T(8,128)}) %reduce-scatter.4.cloned.1.call-update) | async-done | bytes 327696 | tf_op jit(solution)/shard_map/reduce_scatter | solution.py:70
  (113 shorter events, 147.4 us)
Async XLA Ops:
  7.2 237.7 %all-gather.9.cloned.1.call-start = ((), (), s32[]{:S(2)}) async-start(), calls=%async_computation.4 | async-start | bytes 1474560 | tf_op jit(solution)/shard_map/all_gather | solution.py:63
  7.9 237.0 %all-gather.13.cloned.1.call-start = ((), (), s32[]{:S(2)}) async-start(), calls=%async_computation.6 | async-start | bytes 1474560 | tf_op jit(solution)/shard_map/all_gather | solution.py:64
  8.6 236.3 %all-gather.7.cloned.1.call-start = ((), (), s32[]{:S(2)}) async-start(), calls=%async_computation.3 | async-start | bytes 5406720 | tf_op jit(solution)/shard_map/all_gather | solution.py:55
  9.4 329.6 %all-gather.11.cloned.1.call-start = ((), (), s32[]{:S(2)}) async-start(), calls=%async_computation.5 | async-start | bytes 5406720 | tf_op jit(solution)/shard_map/all_gather | solution.py:56
  10.0 559.1 %reduce-scatter.8.cloned.1.call-start = ((), (), s32[]{:S(2)}) async-start(), calls=%async_computation.9 | async-start | bytes 2949120 | tf_op jit(solution)/shard_map/reduce_scatter | solution.py:73
  533.6 1.7 copy-start
  533.6 80.1 %reduce-scatter.6.cloned.1.call-start = ((), (), s32[]{:S(2)}) async-start(), calls=%async_computation.8 | async-start | bytes 2949120 | tf_op jit(solution)/shard_map/reduce_scatter | solution.py:72
  537.5 543.5 %reduce-scatter.4.cloned.1.call-start = ((), (), s32[]{:S(2)}) async-start(), calls=%async_computation.7 | async-start | bytes 10813440 | tf_op jit(solution)/shard_map/reduce_scatter | solution.py:70
Sparse Core Ops, SparseCore 0:
  9.8 38.8 all-gather.8
  50.5 38.1 all-gather.12
  92.1 121.3 all-gather.6
  216.8 122.1 all-gather.10
  533.8 35.2 reduce-scatter.7
  571.5 42.2 reduce-scatter.5
  616.3 464.6 reduce-scatter.3
where the time goes:
time: 1100 us; the launch traced here: 1090 us
  waiting for transfers between devices  625 us (57%)
  blocking collectives  230 us (21%)
  matrix products  185 us (17%)
  local copies, waits for them, and re-layouts  27.2 us (2%)
  between operations  14.9 us (1%)
    reduce_scatter x1, waiting for transfers between devices, on_device(): lax.psum_scatter(query_acc, 'col', scatter_dimension=0, tiled=True)  466 us
    all_gather x1, blocking collectives, on_device(): lax.all_gather(delta, 'col', axis=0, tiled=True)  107 us
    all_gather x1, blocking collectives, on_device(): lax.all_gather(saved_lse, 'col', axis=0, tiled=True)  107 us
    all_gather x1, waiting for transfers between devices, on_device(): lax.all_gather(out_grad, 'col', axis=0, tiled=True)  94 us
    reduce_scatter x1, waiting for transfers between devices, on_device(): lax.psum_scatter(key_acc, 'row', scatter_dimension=0, tiled=True)  43.1 us
    dot_general x16, matrix products, one_head(): query_part = jnp.dot(grad_scores, key_h, preferred_element_type=jnp.float32)  42.2 us
    dot_general x16, matrix products, one_head(): jnp.einsum('qk,qd->kd', grad_scores, query_h, preferred_element_type=jnp....  41.1 us
    dot_general x16, matrix products, one_head(): jnp.einsum('qd,kd->qk', query_h, key_h, preferred_element_type=jnp.float32)  37.3 us
  transfers between devices with their start and end apart: 7, of which 4 were waited for; matrix products, arithmetic and copies ran while one was open for 2% of the time, Pallas kernels for 0%

commit v1 on v0

v1 whole, which is shorter than its diff:
```python
import functools

import jax
import jax.numpy as jnp
from jax import lax
from jax.experimental import pallas as pl
from jax.experimental.pallas import tpu as pltpu
from jax.sharding import PartitionSpec as P

HEADS, DIM, TOK = 16, 80, 64
WIDTH = HEADS * DIM
RING = 4
GROUP = HEADS * TOK
TOKENS = RING * GROUP
PAIR = 2 * TOK
QROWS, KROWS, BACK = 96, 80, 128
SCALING = DIM**-0.5
LOG2E = 1.4426950408889634
MESH = pl.DeviceIdType.MESH
F32, BF16 = jnp.float32, jnp.bfloat16
VMEM = pl.BlockSpec(memory_space=pltpu.VMEM)
LIMIT = 56 * 2**20


def place():
    row, col = lax.axis_index("row"), lax.axis_index("col")
    high = lax.rem(col, 2)
    x = lax.rem(lax.div(col, 2), RING)
    y = lax.div(col, 2 * RING)
    return row, col, high * 8 + row, x, y


def head_device(col, head):
    return (lax.rem(head, 8), col - lax.rem(col, 2) + lax.div(head, 8))


def x_device(row, col, x, other):
    return (row, col + 2 * (other - x))


def y_device(row, col, y, other):
    return (row, col + 2 * RING * (other - y))


def greet(devices):
    barrier = pltpu.get_barrier_semaphore()
    for device in devices:
        pl.semaphore_signal(barrier, inc=1, device_id=device, device_id_type=MESH)
    pl.semaphore_wait(barrier, len(devices))


def prepare(q_ref, g_ref, o_ref, k_ref, v_ref, lse_ref, keep_ref, qg_ref, kv_ref):
    def flip(top, bottom):
        return jnp.concatenate([top, bottom], axis=0).astype(F32).T

    lane = lax.broadcasted_iota(jnp.int32, (HEADS, PAIR), 1)
    qg = flip(q_ref[...], g_ref[...])
    both = flip(o_ref[...], o_ref[...])
    delta = jnp.sum((qg * both).reshape(HEADS, DIM, PAIR), axis=1)
    lse = jnp.concatenate([lse_ref[...], jnp.zeros((TOK, HEADS), F32)], axis=0)
    lse = jnp.concatenate([lse, jnp.zeros((PAIR, PAIR - HEADS), F32)], axis=1).T[:HEADS]
    extra = jnp.where(lane < TOK, lse * (1.0 / SCALING), delta)
    first = extra.astype(BF16).astype(F32)
    second = (extra - first).astype(BF16).astype(F32)
    third = extra - first - second
    line = lax.broadcasted_iota(jnp.int32, (QROWS - DIM, PAIR), 0)
    qg_ref[:, :DIM, :] = qg.astype(BF16).reshape(HEADS, DIM, PAIR)
    for head in range(HEADS):
        rows = jnp.where(line == 0, first[head : head + 1], 0.0)
        rows = jnp.where(line == 1, second[head : head + 1], rows)
        rows = jnp.where(line == 2, third[head : head + 1], rows)
        qg_ref[head, DIM:, :] = rows.astype(BF16)
    kv = flip(k_ref[...], v_ref[...]) * keep_ref[...]
    kv_ref[...] = kv.astype(BF16).reshape(HEADS, DIM, PAIR)


def spread(qg_ref, kv_ref, qs_ref, ks_ref, local_sem, send_sem, recv_sem, ring_send, ring_recv):
    row, col, head, x, y = place()
    right, left = lax.rem(x + 1, RING), lax.rem(x + RING - 1, RING)
    up, down = lax.rem(y + 1, RING), lax.rem(y + RING - 1, RING)
    others = [lax.rem(head + step, HEADS) for step in range(1, HEADS)]
    sides = (
        (qs_ref, x, right, left, lambda other: x_device(row, col, x, other)),
        (ks_ref, y, up, down, lambda other: y_device(row, col, y, other)),
    )
    greet(
        [head_device(col, other) for other in others]
        + [find(other) for _, _, after, before, find in sides for other in (after, before)]
    )
    copies = []
    for which, (source, target, at) in enumerate(((qg_ref, qs_ref, x), (kv_ref, ks_ref, y))):
        for number, other in enumerate(others):
            copy = pltpu.make_async_remote_copy(
                src_ref=source.at[other],
                dst_ref=target.at[at, head],
                send_sem=send_sem.at[which, number],
                recv_sem=recv_sem.at[which, number],
                device_id=head_device(col, other),
                device_id_type=MESH,
            )
            copy.start()
            copies.append(copy)
        own = pltpu.make_async_copy(source.at[head], target.at[at, head], local_sem.at[which])
        own.start()
        copies.append(own)
    for copy in copies:
        copy.wait()

    def ring(which, number, ref, part, device):
        copy = pltpu.make_async_remote_copy(
            src_ref=part,
            dst_ref=part,
            send_sem=ring_send.at[which, number],
            recv_sem=ring_recv.at[which, number],
            device_id=device,
            device_id_type=MESH,
        )
        copy.start()
        return copy

    first = []
    for which, (ref, at, after, before, find) in enumerate(sides):
        first.append(
            (
                ring(which, 0, ref, ref.at[at], find(after)),
                ring(which, 1, ref, ref.at[at], find(before)),
            )
        )
    second = []
    half = HEADS // 2
    for which, (ref, at, after, before, find) in enumerate(sides):
        first[which][0].wait()
        second.append(ring(which, 2, ref, ref.at[before, pl.ds(0, half)], find(after)))
        first[which][1].wait()
        second.append(ring(which, 3, ref, ref.at[after, pl.ds(half, half)], find(before)))
    for copy in second:
        copy.wait()


def attend(qs_ref, ks_ref, dq_ref, dk_ref, dv_ref, own_q, own_k, own_v, qa, ga, qt, gt, ka, va, kt, acc):
    _, _, _, x, y = place()
    lane = lax.broadcasted_iota(jnp.int32, (1, PAIR), 1)
    low = lane < TOK

    def split(one, two):
        return (
            jnp.where(low, one, pltpu.roll(two, TOK, 1)),
            jnp.where(low, pltpu.roll(one, TOK, 1), two),
        )

    minus = jnp.where(lax.broadcasted_iota(jnp.int32, (QROWS - DIM, PAIR), 0) < 3, -1.0, 0.0)
    fill = jnp.zeros((PAIR - QROWS, PAIR), F32)

    @pl.loop(0, RING * HEADS // 2)
    def _(pair):
        at = lax.div(pair, HEADS // 2)
        one, two = 2 * lax.rem(pair, HEADS // 2), 2 * lax.rem(pair, HEADS // 2) + 1
        here = pl.ds(pl.multiple_of(pair * PAIR, PAIR), PAIR)
        q, g = split(qs_ref[at, one].astype(F32), qs_ref[at, two].astype(F32))
        qt[:, here] = q[:DIM].astype(BF16)
        gt[:, here] = g[:DIM].astype(BF16)
        qa[here, :] = jnp.concatenate([q, fill], axis=0).T.astype(BF16)
        ga[here, :] = jnp.concatenate([g, fill], axis=0).T.astype(BF16)
        k, v = split(ks_ref[at, one].astype(F32), ks_ref[at, two].astype(F32))
        kt[:, here] = k.astype(BF16)
        ka[:, here] = jnp.concatenate([k, minus, fill], axis=0).astype(BF16)
        va[:, here] = jnp.concatenate([v, minus, fill], axis=0).astype(BF16)

    acc[...] = jnp.zeros_like(acc)
    tq, tk = 1024, 1024

    @pl.loop(0, RING)
    def _(j):
        keys = pl.ds(pl.multiple_of(j * tk, tk), tk)

        def step(i, carry):
            sum_k, sum_v = carry
            queries = pl.ds(pl.multiple_of(i * tq, tq), tq)
            scores = jnp.dot(qa[queries, :], ka[:, keys], preferred_element_type=F32)
            probs = jnp.exp2(scores * (SCALING * LOG2E))
            grad_probs = jnp.dot(ga[queries, :], va[:, keys], preferred_element_type=F32)
            grad_scores = (probs * grad_probs).astype(BF16)
            sum_v = sum_v + jnp.dot(gt[:, queries], probs.astype(BF16), preferred_element_type=F32)
            sum_k = sum_k + jnp.dot(qt[:, queries], grad_scores, preferred_element_type=F32)
            acc[i] += lax.dot_general(
                kt[:, keys], grad_scores, (((1,), (1,)), ((), ())), preferred_element_type=F32
            )
            return sum_k, sum_v

        zeros = jnp.zeros((DIM, tk), F32)
        sum_k, sum_v = lax.fori_loop(0, RING, step, (zeros, zeros))
        dk_ref[j] = sum_k.astype(BF16)
        dv_ref[j] = sum_v.astype(BF16)

        @pl.when(j == y)
        def _():
            own_k[...] = sum_k
            own_v[...] = sum_v

    dq_ref[...] = acc[...].astype(BF16)
    own_q[...] = acc[x]


def collect(
    dq_ref, dk_ref, dv_ref, own_q, own_k, own_v, out_ref,
    got, packed, local_sem, part_send, part_recv, send_sem, recv_sem,
):
    row, col, head, x, y = place()
    others = [lax.rem(head + step, HEADS) for step in range(1, HEADS)]
    xs = [lax.rem(x + step, RING) for step in range(1, RING)]
    ys = [lax.rem(y + step, RING) for step in range(1, RING)]
    greet(
        [head_device(col, other) for other in others]
        + [x_device(row, col, x, other) for other in xs]
        + [y_device(row, col, y, other) for other in ys]
    )
    copies = []
    for which, (ref, places, find) in enumerate(
        (
            (dk_ref, ys, lambda other: y_device(row, col, y, other)),
            (dv_ref, ys, lambda other: y_device(row, col, y, other)),
            (dq_ref, xs, lambda other: x_device(row, col, x, other)),
        )
    ):
        for number, other in enumerate(places):
            copy = pltpu.make_async_remote_copy(
                src_ref=ref.at[other],
                dst_ref=got.at[which, number],
                send_sem=part_send.at[which, number],
                recv_sem=part_recv.at[which, number],
                device_id=find(other),
                device_id_type=MESH,
            )
            copy.start()
            copies.append(copy)
    for copy in copies:
        copy.wait()
    low = lax.broadcasted_iota(jnp.int32, (1, PAIR), 1) < TOK
    fill = jnp.zeros((2 * (BACK - DIM) - DIM, PAIR), F32)

    @pl.loop(0, HEADS // 2)
    def _(pair):
        here = pl.ds(pl.multiple_of(pair * PAIR, PAIR), PAIR)

        def total(which, own):
            value = own[:, here]
            for number in range(RING - 1):
                value = value + got[which, number, :, here].astype(F32)
            return value

        k = total(0, own_k) * SCALING
        v = total(1, own_v)
        q = total(2, own_q) * SCALING
        q_top, q_rest = q[: BACK - DIM], jnp.concatenate([q[BACK - DIM :], fill], axis=0)

        def join(one, two):
            return (
                jnp.where(low, one, pltpu.roll(two, TOK, 1)).astype(BF16),
                jnp.where(low, pltpu.roll(one, TOK, 1), two).astype(BF16),
            )

        kv_one, kv_two = join(k, v)
        q_one, q_two = join(q_top, q_rest)
        packed[2 * pair, :DIM, :] = kv_one
        packed[2 * pair, DIM:, :] = q_one
        packed[2 * pair + 1, :DIM, :] = kv_two
        packed[2 * pair + 1, DIM:, :] = q_two

    copies = []
    for number, other in enumerate(others):
        copy = pltpu.make_async_remote_copy(
            src_ref=packed.at[other],
            dst_ref=out_ref.at[head],
            send_sem=send_sem.at[number],
            recv_sem=recv_sem.at[number],
            device_id=head_device(col, other),
            device_id_type=MESH,
        )
        copy.start()
        copies.append(copy)
    own = pltpu.make_async_copy(packed.at[head], out_ref.at[head], local_sem)
    own.start()
    copies.append(own)
    for copy in copies:
        copy.wait()


def finish(back_ref, keep_ref, dq_ref, dk_ref, dv_ref):
    keep = keep_ref[...]
    keep = keep * pltpu.roll(keep, TOK, 1)
    blocks = back_ref[...].astype(F32)
    kv = blocks[:, :DIM, :].reshape(WIDTH, PAIR) * keep
    kv = kv.T
    dk_ref[...] = kv[:TOK].astype(BF16)
    dv_ref[...] = kv[TOK:].astype(BF16)
    pieces = []
    for head in range(HEADS):
        pieces.append(blocks[head, DIM:, :])
        pieces.append(pltpu.roll(blocks[head, DIM : 3 * DIM - BACK, :], TOK, 1))
    q = jnp.concatenate(pieces, axis=0).T
    dq_ref[...] = q[:TOK].astype(BF16)


def params(**more):
    return pltpu.CompilerParams(vmem_limit_bytes=LIMIT, **more)


def on_device(query_vecs, key_vecs, value_vecs, attn_out, out_grad, saved_lse, kept_mask):
    shape = jax.ShapeDtypeStruct
    keep = jnp.concatenate([kept_mask.astype(F32), jnp.ones((TOK,), F32)]).reshape(1, PAIR)
    qg, kv = pl.pallas_call(
        prepare,
        out_shape=[shape((HEADS, QROWS, PAIR), BF16), shape((HEADS, KROWS, PAIR), BF16)],
        in_specs=[VMEM] * 7,
        out_specs=[VMEM] * 2,
        compiler_params=params(),
    )(query_vecs, out_grad, attn_out, key_vecs, value_vecs, saved_lse, keep)
    qs, ks = pl.pallas_call(
        spread,
        out_shape=[shape((RING, HEADS, QROWS, PAIR), BF16), shape((RING, HEADS, KROWS, PAIR), BF16)],
        in_specs=[VMEM] * 2,
        out_specs=[VMEM] * 2,
        scratch_shapes=[
            pltpu.SemaphoreType.DMA((2,)),
            pltpu.SemaphoreType.DMA((2, HEADS - 1)),
            pltpu.SemaphoreType.DMA((2, HEADS - 1)),
            pltpu.SemaphoreType.DMA((2, 4)),
            pltpu.SemaphoreType.DMA((2, 4)),
        ],
        compiler_params=params(collective_id=0, has_side_effects=True),
    )(qg, kv)
    part = shape((RING, DIM, GROUP), BF16)
    own = shape((DIM, GROUP), F32)
    parts = pl.pallas_call(
        attend,
        out_shape=[part] * 3 + [own] * 3,
        in_specs=[VMEM] * 2,
        out_specs=[VMEM] * 6,
        scratch_shapes=[
            pltpu.VMEM((TOKENS, PAIR), BF16),
            pltpu.VMEM((TOKENS, PAIR), BF16),
            pltpu.VMEM((DIM, TOKENS), BF16),
            pltpu.VMEM((DIM, TOKENS), BF16),
            pltpu.VMEM((PAIR, TOKENS), BF16),
            pltpu.VMEM((PAIR, TOKENS), BF16),
            pltpu.VMEM((DIM, TOKENS), BF16),
            pltpu.VMEM((RING, DIM, GROUP), F32),
        ],
        compiler_params=params(),
    )(qs, ks)
    back = pl.pallas_call(
        collect,
        out_shape=shape((HEADS, BACK, PAIR), BF16),
        in_specs=[VMEM] * 6,
        out_specs=VMEM,
        scratch_shapes=[
            pltpu.VMEM((3, RING - 1, DIM, GROUP), BF16),
            pltpu.VMEM((HEADS, BACK, PAIR), BF16),
            pltpu.SemaphoreType.DMA,
            pltpu.SemaphoreType.DMA((3, RING - 1)),
            pltpu.SemaphoreType.DMA((3, RING - 1)),
            pltpu.SemaphoreType.DMA((HEADS - 1,)),
            pltpu.SemaphoreType.DMA((HEADS - 1,)),
        ],
        compiler_params=params(collective_id=1, has_side_effects=True),
    )(*parts)
    out = shape((TOK, WIDTH), BF16)
    return pl.pallas_call(
        finish,
        out_shape=[out] * 3,
        in_specs=[VMEM] * 2,
        out_specs=[VMEM] * 3,
        compiler_params=params(),
    )(back, keep)


def solution(mesh):
    queries, keys = P(("row", "col"), None), P(("col", "row"), None)
    return jax.shard_map(
        on_device,
        mesh=mesh,
        in_specs=(queries, keys, keys, queries, queries, queries, P(("col", "row"))),
        out_specs=(queries, keys, keys),
        check_vma=False,
    )
```

time: 1100 us -> 147 us (0.13)
  waiting for transfers between devices: 625 us -> 0 us
  blocking collectives: 230 us -> 0 us
  matrix products: 185 us -> 0 us
  Pallas kernels: 0 us -> 143 us
  local copies, waits for them, and re-layouts: 27.2 us -> 1.9 us
  between operations: 14.9 us -> 0.65 us
    reduce_scatter x3 -> x0, waiting for transfers between devices: 529 us -> none  [the longest x1 466 us: on_device(): lax.psum_scatter(query_acc, 'col', scatter_dimension=0, tiled=True)]
    all_gather x2 -> x0, blocking collectives: 214 us -> none  [the longest x1 107 us: on_device(): lax.all_gather(delta, 'col', axis=0, tiled=True)]
    dot_general x80 -> x0, matrix products: 185 us -> none  [the longest x16 42.2 us: one_head(): query_part = jnp.dot(grad_scores, key_h, preferred_element_type=jnp.float32)]
    pallas_call x0 -> x5, Pallas kernels: none -> 143 us  [the longest x1 52.8 us: on_device(): pl.pallas_call(attend, out_shape=[part] * 3 + [own] * 3, in_specs=[VMEM]...]
    all_gather x4 -> x0, waiting for transfers between devices: 94.1 us -> none  [the longest x1 94 us: on_device(): lax.all_gather(out_grad, 'col', axis=0, tiled=True)]
    unnamed x1 -> x0, blocking collectives: 16.3 us -> none
    while x3 -> x0, local copies, waits for them, and re-layouts: 15.6 us -> none  [attend(): return lax.fori_loop(0, heads, one_head, start)]
  transfers between devices with their start and end apart: 7 -> 0, of which waited for: 4 -> 0; matrix products, arithmetic and copies ran while one was open for 2% -> 0% of each run, Pallas kernels for 0% -> 0%
where the time goes in v1:
time: 147 us
  Pallas kernels  143 us (97%)
  local copies, waits for them, and re-layouts  1.9 us (1%)
    pallas_call x1, Pallas kernels, on_device(): pl.pallas_call(attend, out_shape=[part] * 3 + [own] * 3, in_specs=[VMEM]...  52.8 us
    pallas_call x1, Pallas kernels, on_device(): pl.pallas_call(spread, out_shape=[shape((RING, HEADS, QROWS, PAIR), BF16)...  47 us
    pallas_call x1, Pallas kernels, on_device(): pl.pallas_call(collect, out_shape=shape((HEADS, BACK, PAIR), BF16), in_sp...  39.1 us

profile of v1, /device:TPU:1, one launch (start us, length us, event | category | flops | bytes accessed | tf_op | source)
XLA Modules:
  0.0 146.6 jit_solution(3920856513596261507)
XLA Ops:
  0.6 0.7 convert_element_type.3
  1.3 0.5 pad_bitcast_fusion.keep_ref
  1.8 1.4 copy.10.lse_ref
  3.2 2.4 %shard_map.94 = (bf16[16,96,128]{2,1,0:T(8,128)(2,1)}, bf16[16,80,128]{2,1,0:T(8,128)(2,1)}) custom-call(bf16[64,1280]{1,0:T(8,128)(2,1)} %q_ref.1, bf16[64,1280]{1,0:T(8,128)(2,1)} %g_ref.1, bf16[64,1280]{1,0:T(8,128)(2,1)} %o_ref.1, bf16[64,1280]{1,0:T(8,128)(2,1)} %k_ref.1, bf16[64,1280]{1,0:T(8,128)(2,1)} %v_ref.1, f32[64,16]{1,0:T(8,128)} %copy.10.lse_ref, ...), custom_call_target="tpu_custom_call" | custom-call | tf_op jit(solution)/shard_map/pallas_call | solution.py:311
  5.6 47.0 %shard_map.95 = (bf16[4,16,96,128]{3,2,1,0:T(8,128)(2,1)}, bf16[4,16,80,128]{3,2,1,0:T(8,128)(2,1)}) custom-call(bf16[16,96,128]{2,1,0:T(8,128)(2,1)} %get-tuple-element.13.qg_ref, bf16[16,80,128]{2,1,0:T(8,128)(2,1)} %get-tuple-element.14.kv_ref), custom_call_target="tpu_custom_call" | custom-call | tf_op jit(solution)/shard_map/pallas_call | solution.py:318
  52.6 52.8 %shard_map.96 = (bf16[4,80,1024]{2,1,0:T(8,128)(2,1)}, bf16[4,80,1024]{2,1,0:T(8,128)(2,1)}, bf16[4,80,1024]{2,1,0:T(8,128)(2,1)}, f32[80,1024]{1,0:T(8,128)}, f32[80,1024]{1,0:T(8,128)}, /*index=5*/f32[80,1024]{1,0:T(8,128)}) custom-call(bf16[4,16,96,128]{3,2,1,0:T(8,128)(2,1)} %get-tuple-element.15.qs_ref, bf16[4,16,80,128]{3,2,1,0:T(8,128)(2,1)} %get-tuple-element.16.ks_ref), custom_call_target="tpu_custom_call" | custom-call | tf_op jit(solution)/shard_map/pallas_call | solution.py:334
  105.4 39.1 %shard_map.97.back_ref = bf16[16,128,128]{2,1,0:T(8,128)(2,1)} custom-call(bf16[4,80,1024]{2,1,0:T(8,128)(2,1)} %get-tuple-element.17.dq_ref, bf16[4,80,1024]{2,1,0:T(8,128)(2,1)} %get-tuple-element.18.dk_ref, bf16[4,80,1024]{2,1,0:T(8,128)(2,1)} %get-tuple-element.19.dv_ref, f32[80,1024]{1,0:T(8,128)} %get-tuple-element.20.own_q, ...), custom_call_target="tpu_custom_call" | custom-call | tf_op jit(solution)/shard_map/pallas_call | solution.py:351
  144.5 2.0 %shard_map.98 = (bf16[64,1280]{1,0:T(8,128)(2,1)}, bf16[64,1280]{1,0:T(8,128)(2,1)}, bf16[64,1280]{1,0:T(8,128)(2,1)}) custom-call(bf16[16,128,128]{2,1,0:T(8,128)(2,1)} %shard_map.97.back_ref, f32[1,128]{1,0:T(1,128)} %pad_bitcast_fusion.keep_ref), custom_call_target="tpu_custom_call" | custom-call | tf_op jit(solution)/shard_map/pallas_call | solution.py:368

commit v2 on v0

v2 whole, which is shorter than its diff:
```python
import jax
import jax.numpy as jnp
from jax import lax
from jax.experimental import pallas as pl
from jax.experimental.pallas import tpu as pltpu
from jax.sharding import PartitionSpec as P

HEADS, DIM, TOK = 16, 80, 64
WIDTH = HEADS * DIM
RING = 4
GROUP = HEADS * TOK
PAIR = 2 * TOK
QUARTER = GROUP // RING
QROWS, TOP = 96, 48
REST = DIM - TOP
SCALING = DIM**-0.5
LOG2E = 1.4426950408889634
MESH = pl.DeviceIdType.MESH
F32, BF16 = jnp.float32, jnp.bfloat16
VMEM = pl.BlockSpec(memory_space=pltpu.VMEM)


def kernel(
    q_ref, g_ref, o_ref, k_ref, v_ref, lse_ref, keep_ref, dq_ref, dk_ref, dv_ref,
    keep, extra, qg, kv, qs, ks, qa, ga, qt, gt, ka, va, kt, acc_q, acc_k, acc_v,
    part_k, got_k, own_k, part_q, got_q, pack_k, pack_q, back_k, back_q,
    local_sem, in_send, in_recv, ring_send, ring_recv,
    sum_send, sum_recv, sumq_send, sumq_recv, out_send, out_recv,
):
    row, col = lax.axis_index("row"), lax.axis_index("col")
    high = lax.rem(col, 2)
    head = high * 8 + row
    x, y = lax.rem(lax.div(col, 2), RING), lax.div(col, 2 * RING)

    def head_device(step):
        other = lax.rem(head + step + HEADS, HEADS)
        return other, (lax.rem(other, 8), col - high + lax.div(other, 8))

    def side_device(which, step):
        if which == 0:
            return (row, col + 2 * (lax.rem(x + step + RING, RING) - x))
        return (row, col + 2 * RING * (lax.rem(y + step + RING, RING) - y))

    def remote(source, target, send, recv, device):
        return pltpu.make_async_remote_copy(
            src_ref=source, dst_ref=target, send_sem=send, recv_sem=recv,
            device_id=device, device_id_type=MESH,
        )

    def arrive(which, step):
        other, device = head_device(step)
        source, target = ((qg, qs), (kv, ks))[which]
        return remote(
            source.at[other], target.at[0, step],
            in_send.at[which, step], in_recv.at[which, step], device,
        )

    def arrive_own(which):
        source, target = ((qg, qs), (kv, ks))[which]
        return pltpu.make_async_copy(source.at[head], target.at[0, 0], local_sem.at[which])

    def ring(which, group, kind):
        ref = (qs, ks)[which]
        source, target, first, count, step = (
            (0, 1, 0, 4, 1), (0, 2, 0, 4, -1), (1, 3, 0, 2, 1), (2, 3, 2, 2, -1),
        )[kind]
        part = pl.ds(4 * group + first, count)
        return remote(
            ref.at[source, part], ref.at[target, part],
            ring_send.at[which, group, kind], ring_recv.at[which, group, kind],
            side_device(which, step),
        )

    back_steps = (-1, 1, 2)

    def sum_keys(quarter, slot):
        return remote(
            part_k.at[quarter, slot], got_k.at[quarter, slot],
            sum_send.at[quarter, slot], sum_recv.at[quarter, slot],
            side_device(1, back_steps[slot]),
        )

    def sum_queries(slot):
        return remote(
            part_q.at[slot], got_q.at[slot], sumq_send.at[slot], sumq_recv.at[slot],
            side_device(0, back_steps[slot]),
        )

    def leave(which, step):
        source, target = ((pack_q, back_q), (pack_k, back_k))[which]
        if step == 0:
            return pltpu.make_async_copy(source.at[0], target.at[head], local_sem.at[2 + which])
        _, device = head_device(-step)
        return remote(
            source.at[step], target.at[head],
            out_send.at[which, step], out_recv.at[which, step], device,
        )

    barrier = pltpu.get_barrier_semaphore()
    partners = [head_device(step)[1] for step in range(1, HEADS)]
    partners += [side_device(which, step) for which in (0, 1) for step in back_steps]
    for device in partners:
        pl.semaphore_signal(barrier, inc=1, device_id=device, device_id_type=MESH)

    def flip(top, bottom):
        return jnp.concatenate([top, bottom], axis=0).astype(F32).T

    keep[...] = jnp.ones_like(keep)
    keep[0:1, :TOK] = keep_ref[...].astype(F32)
    kv[...] = (flip(k_ref[...], v_ref[...]) * keep[0:1, :]).astype(BF16).reshape(HEADS, DIM, PAIR)
    pl.semaphore_wait(barrier, len(partners))
    arrive_own(1).start()
    for step in range(1, 4):
        arrive(1, step).start()

    qg_flat = flip(q_ref[...], g_ref[...])
    o_flat = flip(o_ref[...], o_ref[...])
    delta = jnp.sum((qg_flat * o_flat).reshape(HEADS, DIM, PAIR), axis=1)
    extra[...] = jnp.zeros_like(extra)
    extra[:, :TOK] = lse_ref[...] * (1.0 / SCALING)
    low = lax.broadcasted_iota(jnp.int32, (1, PAIR), 1) < TOK
    whole = jnp.where(low, extra[...], delta)
    first = whole.astype(BF16).astype(F32)
    second = (whole - first).astype(BF16).astype(F32)
    third = whole - first - second
    line = lax.broadcasted_iota(jnp.int32, (QROWS - DIM, PAIR), 0)
    qg[:, :DIM, :] = qg_flat.astype(BF16).reshape(HEADS, DIM, PAIR)
    for number in range(HEADS):
        rows = jnp.where(line == 0, first[number : number + 1], 0.0)
        rows = jnp.where(line == 1, second[number : number + 1], rows)
        rows = jnp.where(line == 2, third[number : number + 1], rows)
        qg[number, DIM:, :] = rows.astype(BF16)
    arrive_own(0).start()
    for step in range(1, HEADS):
        arrive(0, step).start()
    for step in range(4, HEADS):
        arrive(1, step).start()

    def swap(value):
        return pltpu.roll(value, TOK, 1)

    def mix(one, two):
        return jnp.where(low, one, swap(two)), jnp.where(low, swap(one), two)

    minus = jnp.where(line < 3, -1.0, 0.0)
    fill = jnp.zeros((PAIR - QROWS, PAIR), F32)

    def lay_queries(slot, pairs):
        for pair in pairs:
            here = pl.ds(pair * PAIR, PAIR)
            q, g = mix(qs[slot, 2 * pair].astype(F32), qs[slot, 2 * pair + 1].astype(F32))
            qt[slot, :, here] = q[:DIM].astype(BF16)
            gt[slot, :, here] = g[:DIM].astype(BF16)
            qa[slot, here, :] = jnp.concatenate([q, fill], axis=0).T.astype(BF16)
            ga[slot, here, :] = jnp.concatenate([g, fill], axis=0).T.astype(BF16)

    def lay_keys(quarter, slot):
        for pair in range(2):
            here = pl.ds(slot * QUARTER + pair * PAIR, PAIR)
            at = 4 * quarter + 2 * pair
            k, v = mix(ks[slot, at].astype(F32), ks[slot, at + 1].astype(F32))
            kt[quarter, :, here] = k.astype(BF16)
            ka[quarter, :, here] = jnp.concatenate([k, minus, fill], axis=0).astype(BF16)
            va[quarter, :, here] = jnp.concatenate([v, minus, fill], axis=0).astype(BF16)

    def ring_one(which, group):
        for step in range(4 * group, 4 * group + 4):
            if step == 0:
                arrive_own(which).wait()
            else:
                arrive(which, step).wait_recv()
        ring(which, group, 0).start()
        ring(which, group, 1).start()

    def ring_two(which, group):
        ring(which, group, 0).wait_recv()
        ring(which, group, 2).start()
        ring(which, group, 1).wait_recv()
        ring(which, group, 3).start()

    def ring_end(which, group):
        ring(which, group, 2).wait_recv()
        ring(which, group, 3).wait_recv()

    def send_keys(quarter):
        for slot in range(3):
            here = pl.ds((slot + 1) * QUARTER, QUARTER)
            part_k[quarter, slot, 0] = acc_k[:, here].astype(BF16)
            part_k[quarter, slot, 1] = acc_v[:, here].astype(BF16)
            sum_keys(quarter, slot).start()
        own_k[quarter, 0] = acc_k[:, :QUARTER]
        own_k[quarter, 1] = acc_v[:, :QUARTER]
        acc_k[...] = jnp.zeros_like(acc_k)
        acc_v[...] = jnp.zeros_like(acc_v)

    def return_keys(quarter):
        for slot in range(3):
            sum_keys(quarter, slot).wait_recv()
        for pair in range(2):
            here = pl.ds(pair * PAIR, PAIR)
            k, v = [
                own_k[quarter, which, :, here]
                + got_k[quarter, 0, which, :, here].astype(F32)
                + got_k[quarter, 1, which, :, here].astype(F32)
                + got_k[quarter, 2, which, :, here].astype(F32)
                for which in (0, 1)
            ]
            one, two = (k * SCALING), v
            at = 4 * quarter + 2 * pair
            pack_k[at] = jnp.where(low, one, swap(two)).astype(BF16)
            pack_k[at + 1] = jnp.where(low, swap(one), two).astype(BF16)
        for step in range(4 * quarter, 4 * quarter + 4):
            leave(1, step).start()

    def send_queries(slot):
        part_q[slot - 1] = acc_q[slot].astype(BF16)
        sum_queries(slot - 1).start()

    def return_queries():
        for slot in range(3):
            sum_queries(slot).wait_recv()
        for pair in range(HEADS // 2):
            here = pl.ds(pair * PAIR, PAIR)
            q = acc_q[0, :, here]
            for slot in range(3):
                q = q + got_q[slot, :, here].astype(F32)
            q = q * SCALING
            one, two = q[:TOP], jnp.concatenate([q[TOP:], jnp.zeros((TOP - REST, PAIR), F32)], axis=0)
            pack_q[2 * pair] = jnp.where(low, one, swap(two)).astype(BF16)
            pack_q[2 * pair + 1] = jnp.where(low, swap(one), two).astype(BF16)
        for step in range(HEADS):
            leave(0, step).start()

    acc_q[...] = jnp.zeros_like(acc_q)
    acc_k[...] = jnp.zeros_like(acc_k)
    acc_v[...] = jnp.zeros_like(acc_v)
    ring_one(1, 0)
    for group in range(4):
        ring_one(0, group)
        lay_queries(0, (2 * group, 2 * group + 1))
    ring_two(1, 0)
    for slot in range(3):
        lay_keys(0, slot)
    ring_end(1, 0)
    lay_keys(0, 3)

    def before(turn):
        quarter, slot = divmod(turn, 4)
        if turn == 1:
            for group in range(4):
                ring_two(0, group)
            for place in (1, 2):
                lay_queries(place, range(HEADS // 2))
        if turn == 3:
            for group in range(4):
                ring_end(0, group)
            lay_queries(3, range(HEADS // 2))
        if slot == 0 and quarter > 0:
            send_keys(quarter - 1)
            ring_end(1, quarter)
            for place in range(4):
                lay_keys(quarter, place)
        if slot == 1 and quarter < 3:
            ring_one(1, quarter + 1)
        if slot == 2 and quarter < 3:
            ring_two(1, quarter + 1)
        if slot == 2 and quarter > 0:
            return_keys(quarter - 1)
        if quarter == 3 and slot > 0:
            send_queries(slot)

    def tile(turn, carry):
        quarter = lax.div(turn, 4)
        slot = lax.rem(turn + lax.div(quarter, 3), 4)
        for at in range(16):
            if at > 0:
                pl.when(turn == at)(lambda at=at: before(at))
        scores = jnp.dot(qa[slot], ka[quarter], preferred_element_type=F32)
        probs = jnp.exp2(scores * (SCALING * LOG2E))
        grad_probs = jnp.dot(ga[slot], va[quarter], preferred_element_type=F32)
        grad_scores = (probs * grad_probs).astype(BF16)
        acc_v[...] += jnp.dot(gt[slot], probs.astype(BF16), preferred_element_type=F32)
        acc_k[...] += jnp.dot(qt[slot], grad_scores, preferred_element_type=F32)
        acc_q[slot] += lax.dot_general(
            kt[quarter], grad_scores, (((1,), (1,)), ((), ())), preferred_element_type=F32
        )
        return carry

    lax.fori_loop(0, 16, tile, 0)
    send_keys(3)
    return_queries()
    return_keys(3)

    for step in range(HEADS):
        for which in (0, 1):
            if step == 0:
                leave(which, step).wait()
            else:
                leave(which, step).wait_recv()
    both = keep[0:1, :] * swap(keep[...])[0:1, :]
    flat = (back_k[...].astype(F32).reshape(WIDTH, PAIR) * both).T
    dk_ref[...] = flat[:TOK].astype(BF16)
    dv_ref[...] = flat[TOK:].astype(BF16)
    pieces = []
    for number in range(HEADS):
        block = back_q[number].astype(F32)
        pieces += [block, swap(block)[:REST]]
    dq_ref[...] = jnp.concatenate(pieces, axis=0).T[:TOK].astype(BF16)

    for step in range(1, HEADS):
        for which in (0, 1):
            arrive(which, step).wait_send()
            leave(which, step).wait_send()
    for which in (0, 1):
        for group in range(4):
            for kind in range(4):
                ring(which, group, kind).wait_send()
    for slot in range(3):
        sum_queries(slot).wait_send()
        for quarter in range(4):
            sum_keys(quarter, slot).wait_send()


def on_device(query_vecs, key_vecs, value_vecs, attn_out, out_grad, saved_lse, kept_mask):
    out = jax.ShapeDtypeStruct((TOK, WIDTH), BF16)
    dma = pltpu.SemaphoreType.DMA

    def low_bits(*dims):
        return pltpu.VMEM(dims, BF16)

    def full(*dims):
        return pltpu.VMEM(dims, F32)

    return pl.pallas_call(
        kernel,
        out_shape=[out] * 3,
        in_specs=[VMEM] * 7,
        out_specs=[VMEM] * 3,
        scratch_shapes=[
            full(8, PAIR),
            full(HEADS, PAIR),
            low_bits(HEADS, QROWS, PAIR),
            low_bits(HEADS, DIM, PAIR),
            low_bits(RING, HEADS, QROWS, PAIR),
            low_bits(RING, HEADS, DIM, PAIR),
            low_bits(RING, GROUP, PAIR),
            low_bits(RING, GROUP, PAIR),
            low_bits(RING, DIM, GROUP),
            low_bits(RING, DIM, GROUP),
            low_bits(RING, PAIR, GROUP),
            low_bits(RING, PAIR, GROUP),
            low_bits(RING, DIM, GROUP),
            full(RING, DIM, GROUP),
            full(DIM, GROUP),
            full(DIM, GROUP),
            low_bits(RING, 3, 2, DIM, QUARTER),
            low_bits(RING, 3, 2, DIM, QUARTER),
            full(RING, 2, DIM, QUARTER),
            low_bits(3, DIM, GROUP),
            low_bits(3, DIM, GROUP),
            low_bits(HEADS, DIM, PAIR),
            low_bits(HEADS, TOP, PAIR),
            low_bits(HEADS, DIM, PAIR),
            low_bits(HEADS, TOP, PAIR),
            dma((4,)),
            dma((2, HEADS)),
            dma((2, HEADS)),
            dma((2, 4, 4)),
            dma((2, 4, 4)),
            dma((4, 3)),
            dma((4, 3)),
            dma((3,)),
            dma((3,)),
            dma((2, HEADS)),
            dma((2, HEADS)),
        ],
        compiler_params=pltpu.CompilerParams(
            vmem_limit_bytes=56 * 2**20, collective_id=0, has_side_effects=True
        ),
    )(
        query_vecs, out_grad, attn_out, key_vecs, value_vecs, saved_lse.T,
        kept_mask.reshape(1, TOK),
    )


def solution(mesh):
    queries, keys = P(("row", "col"), None), P(("col", "row"), None)
    return jax.shard_map(
        on_device,
        mesh=mesh,
        in_specs=(queries, keys, keys, queries, queries, queries, P(("col", "row"))),
        out_specs=(queries, keys, keys),
        check_vma=False,
    )
```

time: 1100 us -> 99.6 us (0.09)
  waiting for transfers between devices: 625 us -> 0 us
  blocking collectives: 230 us -> 0 us
  matrix products: 185 us -> 0 us
  Pallas kernels: 0 us -> 95.5 us
  local copies, waits for them, and re-layouts: 27.2 us -> 3.28 us
  between operations: 14.9 us -> 0.65 us
    reduce_scatter x3 -> x0, waiting for transfers between devices: 529 us -> none  [the longest x1 466 us: on_device(): lax.psum_scatter(query_acc, 'col', scatter_dimension=0, tiled=True)]
    all_gather x2 -> x0, blocking collectives: 214 us -> none  [the longest x1 107 us: on_device(): lax.all_gather(delta, 'col', axis=0, tiled=True)]
    dot_general x80 -> x0, matrix products: 185 us -> none  [the longest x16 42.2 us: one_head(): query_part = jnp.dot(grad_scores, key_h, preferred_element_type=jnp.float32)]
    pallas_call x0 -> x1, Pallas kernels: none -> 95.5 us  [on_device(): pl.pallas_call(kernel, out_shape=[out] * 3, in_specs=[VMEM] * 7, out_spec...]
    all_gather x4 -> x0, waiting for transfers between devices: 94.1 us -> none  [the longest x1 94 us: on_device(): lax.all_gather(out_grad, 'col', axis=0, tiled=True)]
    unnamed x1 -> x0, blocking collectives: 16.3 us -> none
    while x3 -> x0, local copies, waits for them, and re-layouts: 15.6 us -> none  [attend(): return lax.fori_loop(0, heads, one_head, start)]
  transfers between devices with their start and end apart: 7 -> 0, of which waited for: 4 -> 0; matrix products, arithmetic and copies ran while one was open for 2% -> 0% of each run, Pallas kernels for 0% -> 0%
where the time goes in v2:
time: 99.6 us; the launch traced here: 99.4 us
  Pallas kernels  95.5 us (96%)
  local copies, waits for them, and re-layouts  3.28 us (3%)
    pallas_call x1, Pallas kernels, on_device(): pl.pallas_call(kernel, out_shape=[out] * 3, in_specs=[VMEM] * 7, out_spec...  95.5 us
    unnamed x7, local copies, waits for them, and re-layouts  3.28 us

profile of v2, /device:TPU:1, one launch (start us, length us, event | category | flops | bytes accessed | tf_op | source)
XLA Modules:
  0.0 99.4 jit_solution(3999193644159812425)
XLA Ops:
  0.6 95.5 %shard_map.94 = (bf16[64,1280]{1,0:T(8,128)(2,1)}, bf16[64,1280]{1,0:T(8,128)(2,1)}, bf16[64,1280]{1,0:T(8,128)(2,1)}) custom-call(bf16[64,1280]{1,0:T(8,128)(2,1)} %q_ref.1, bf16[64,1280]{1,0:T(8,128)(2,1)} %g_ref.1, bf16[64,1280]{1,0:T(8,128)(2,1)} %o_ref.1, bf16[64,1280]{1,0:T(8,128)(2,1)} %k_ref.1, bf16[64,1280]{1,0:T(8,128)(2,1)} %v_ref.1, ...), custom_call_target="tpu_custom_call" | custom-call | tf_op jit(solution)/shard_map/pallas_call | solution.py:334
  96.2 0.0 copy-start.1
  96.2 1.6 %copy.13 = bf16[64,1280]{1,0:T(8,128)(2,1)} copy(bf16[64,1280]{1,0:T(8,128)(2,1)} %get-tuple-element.6) | data formatting | bytes 327680
  97.8 0.0 copy-done.1
  97.8 0.0 copy-start
  97.8 0.7 copy.14
  98.5 0.3 copy-done
  98.8 0.7 copy.15
Async XLA Ops:
  96.2 1.6 %copy-start.1 = (bf16[64,1280]{1,0:T(8,128)(2,1)S(1)}, bf16[64,1280]{1,0:T(8,128)(2,1)}, u32[]{:S(2)}) copy-start(bf16[64,1280]{1,0:T(8,128)(2,1)} %get-tuple-element.7) | copy-start | bytes 491524
  97.8 1.0 copy-start

commit v3 on v2

--- a/solution.py
+++ b/solution.py
@@ -17,13 +17,20 @@
 LOG2E = 1.4426950408889634
 MESH = pl.DeviceIdType.MESH
 F32, BF16 = jnp.float32, jnp.bfloat16
+STEPS = (0, 1, -1, 2, -2, 3, -3, 4, -4, 5, -5, 6, -6, 7, -7, 8)
+ORDER = (
+    (0, 0), (0, 1), (1, 0), (1, 1), (0, 2), (1, 2), (2, 0), (2, 1), (2, 2),
+    (3, 3), (0, 3), (1, 3), (2, 3), (3, 1), (3, 2), (3, 0),
+)
+QUERY_CODE = sum((3 - q) * 4**turn for turn, (q, _) in enumerate(ORDER))
+KEY_CODE = sum(k * 4**turn for turn, (_, k) in enumerate(ORDER))
 VMEM = pl.BlockSpec(memory_space=pltpu.VMEM)
 
 
 def kernel(
     q_ref, g_ref, o_ref, k_ref, v_ref, lse_ref, keep_ref, dq_ref, dk_ref, dv_ref,
     keep, extra, qg, kv, qs, ks, qa, ga, qt, gt, ka, va, kt, acc_q, acc_k, acc_v,
-    part_k, got_k, own_k, part_q, got_q, pack_k, pack_q, back_k, back_q,
+    part_k, got_k, part_q, got_q, pack_k, pack_q, back_k, back_q,
     local_sem, in_send, in_recv, ring_send, ring_recv,
     sum_send, sum_recv, sumq_send, sumq_recv, out_send, out_recv,
 ):
@@ -48,7 +55,7 @@
         )
 
     def arrive(which, step):
-        other, device = head_device(step)
+        other, device = head_device(STEPS[step])
         source, target = ((qg, qs), (kv, ks))[which]
         return remote(
             source.at[other], target.at[0, step],
@@ -80,9 +87,10 @@
             side_device(1, back_steps[slot]),
         )
 
-    def sum_queries(slot):
+    def sum_queries(quarter, slot):
         return remote(
-            part_q.at[slot], got_q.at[slot], sumq_send.at[slot], sumq_recv.at[slot],
+            part_q.at[quarter, slot], got_q.at[quarter, slot],
+            sumq_send.at[quarter, slot], sumq_recv.at[quarter, slot],
             side_device(0, back_steps[slot]),
         )
 
@@ -90,7 +98,7 @@
         source, target = ((pack_q, back_q), (pack_k, back_k))[which]
         if step == 0:
             return pltpu.make_async_copy(source.at[0], target.at[head], local_sem.at[2 + which])
-        _, device = head_device(-step)
+        _, device = head_device(-STEPS[step])
         return remote(
             source.at[step], target.at[head],
             out_send.at[which, step], out_recv.at[which, step], device,
@@ -108,10 +116,6 @@
     keep[...] = jnp.ones_like(keep)
     keep[0:1, :TOK] = keep_ref[...].astype(F32)
     kv[...] = (flip(k_ref[...], v_ref[...]) * keep[0:1, :]).astype(BF16).reshape(HEADS, DIM, PAIR)
-    pl.semaphore_wait(barrier, len(partners))
-    arrive_own(1).start()
-    for step in range(1, 4):
-        arrive(1, step).start()
 
     qg_flat = flip(q_ref[...], g_ref[...])
     o_flat = flip(o_ref[...], o_ref[...])
@@ -130,11 +134,13 @@
         rows = jnp.where(line == 1, second[number : number + 1], rows)
         rows = jnp.where(line == 2, third[number : number + 1], rows)
         qg[number, DIM:, :] = rows.astype(BF16)
-    arrive_own(0).start()
-    for step in range(1, HEADS):
-        arrive(0, step).start()
-    for step in range(4, HEADS):
-        arrive(1, step).start()
+    pl.semaphore_wait(barrier, len(partners))
+    for which in (0, 1):
+        arrive_own(which).start()
+    for group in range(4):
+        for which in (0, 1):
+            for step in range(max(1, 4 * group), 4 * group + 4):
+                arrive(which, step).start()
 
     def swap(value):
         return pltpu.roll(value, TOK, 1)
@@ -145,14 +151,15 @@
     minus = jnp.where(line < 3, -1.0, 0.0)
     fill = jnp.zeros((PAIR - QROWS, PAIR), F32)
 
-    def lay_queries(slot, pairs):
-        for pair in pairs:
-            here = pl.ds(pair * PAIR, PAIR)
-            q, g = mix(qs[slot, 2 * pair].astype(F32), qs[slot, 2 * pair + 1].astype(F32))
-            qt[slot, :, here] = q[:DIM].astype(BF16)
-            gt[slot, :, here] = g[:DIM].astype(BF16)
-            qa[slot, here, :] = jnp.concatenate([q, fill], axis=0).T.astype(BF16)
-            ga[slot, here, :] = jnp.concatenate([g, fill], axis=0).T.astype(BF16)
+    def lay_queries(quarter, slot):
+        for pair in range(2):
+            here = pl.ds(slot * QUARTER + pair * PAIR, PAIR)
+            at = 4 * quarter + 2 * pair
+            q, g = mix(qs[slot, at].astype(F32), qs[slot, at + 1].astype(F32))
+            qt[quarter, :, here] = q[:DIM].astype(BF16)
+            gt[quarter, :, here] = g[:DIM].astype(BF16)
+            qa[quarter, here, :] = jnp.concatenate([q, fill], axis=0).T.astype(BF16)
+            ga[quarter, here, :] = jnp.concatenate([g, fill], axis=0).T.astype(BF16)
 
     def lay_keys(quarter, slot):
         for pair in range(2):
@@ -163,133 +170,148 @@
             ka[quarter, :, here] = jnp.concatenate([k, minus, fill], axis=0).astype(BF16)
             va[quarter, :, here] = jnp.concatenate([v, minus, fill], axis=0).astype(BF16)
 
-    def ring_one(which, group):
-        for step in range(4 * group, 4 * group + 4):
-            if step == 0:
-                arrive_own(which).wait()
-            else:
-                arrive(which, step).wait_recv()
-        ring(which, group, 0).start()
-        ring(which, group, 1).start()
-
-    def ring_two(which, group):
-        ring(which, group, 0).wait_recv()
-        ring(which, group, 2).start()
-        ring(which, group, 1).wait_recv()
-        ring(which, group, 3).start()
-
-    def ring_end(which, group):
-        ring(which, group, 2).wait_recv()
-        ring(which, group, 3).wait_recv()
+    def ring_one(group):
+        for which in (0, 1):
+            for step in range(4 * group, 4 * group + 4):
+                if step == 0:
+                    arrive_own(which).wait()
+                else:
+                    arrive(which, step).wait_recv()
+            ring(which, group, 0).start()
+            ring(which, group, 1).start()
+
+    def ring_two(group):
+        for which in (0, 1):
+            ring(which, group, 0).wait_recv()
+            ring(which, group, 2).start()
+            ring(which, group, 1).wait_recv()
+            ring(which, group, 3).start()
+
+    def ring_end(group):
+        for which in (0, 1):
+            ring(which, group, 2).wait_recv()
+            ring(which, group, 3).wait_recv()
+
+    def lay(group, slots):
+        for slot in slots:
+            lay_queries(group, slot)
+            lay_keys(group, slot)
 
     def send_keys(quarter):
         for slot in range(3):
             here = pl.ds((slot + 1) * QUARTER, QUARTER)
-            part_k[quarter, slot, 0] = acc_k[:, here].astype(BF16)
-            part_k[quarter, slot, 1] = acc_v[:, here].astype(BF16)
+            part_k[quarter, slot, 0] = acc_k[quarter, :, here].astype(BF16)
+            part_k[quarter, slot, 1] = acc_v[quarter, :, here].astype(BF16)
             sum_keys(quarter, slot).start()
-        own_k[quarter, 0] = acc_k[:, :QUARTER]
-        own_k[quarter, 1] = acc_v[:, :QUARTER]
-        acc_k[...] = jnp.zeros_like(acc_k)
-        acc_v[...] = jnp.zeros_like(acc_v)
+
+    def send_queries(quarter):
+        for slot in range(3):
+            here = pl.ds((slot + 1) * QUARTER, QUARTER)
+            part_q[quarter, slot] = acc_q[quarter, :, here].astype(BF16)
+            sum_queries(quarter, slot).start()
 
     def return_keys(quarter):
         for slot in range(3):
             sum_keys(quarter, slot).wait_recv()
         for pair in range(2):
             here = pl.ds(pair * PAIR, PAIR)
-            k, v = [
-                own_k[quarter, which, :, here]
-                + got_k[quarter, 0, which, :, here].astype(F32)
-                + got_k[quarter, 1, which, :, here].astype(F32)
-                + got_k[quarter, 2, which, :, here].astype(F32)
-                for which in (0, 1)
-            ]
-            one, two = (k * SCALING), v
+            k, v = acc_k[quarter, :, here], acc_v[quarter, :, here]
+            for slot in range(3):
+                k = k + got_k[quarter, slot, 0, :, here].astype(F32)
+                v = v + got_k[quarter, slot, 1, :, here].astype(F32)
+            one, two = mix(k * SCALING, v)
             at = 4 * quarter + 2 * pair
-            pack_k[at] = jnp.where(low, one, swap(two)).astype(BF16)
-            pack_k[at + 1] = jnp.where(low, swap(one), two).astype(BF16)
+            pack_k[at] = one.astype(BF16)
+            pack_k[at + 1] = two.astype(BF16)
         for step in range(4 * quarter, 4 * quarter + 4):
             leave(1, step).start()
 
-    def send_queries(slot):
-        part_q[slot - 1] = acc_q[slot].astype(BF16)
-        sum_queries(slot - 1).start()
-
-    def return_queries():
+    def return_queries(quarter):
         for slot in range(3):
-            sum_queries(slot).wait_recv()
-        for pair in range(HEADS // 2):
+            sum_queries(quarter, slot).wait_recv()
+        for pair in range(2):
             here = pl.ds(pair * PAIR, PAIR)
-            q = acc_q[0, :, here]
+            q = acc_q[quarter, :, here]
             for slot in range(3):
-                q = q + got_q[slot, :, here].astype(F32)
+                q = q + got_q[quarter, slot, :, here].astype(F32)
             q = q * SCALING
-            one, two = q[:TOP], jnp.concatenate([q[TOP:], jnp.zeros((TOP - REST, PAIR), F32)], axis=0)
-            pack_q[2 * pair] = jnp.where(low, one, swap(two)).astype(BF16)
-            pack_q[2 * pair + 1] = jnp.where(low, swap(one), two).astype(BF16)
-        for step in range(HEADS):
+            rest = jnp.concatenate([q[TOP:], jnp.zeros((TOP - REST, PAIR), F32)], axis=0)
+            one, two = mix(q[:TOP], rest)
+            at = 4 * quarter + 2 * pair
+            pack_q[at] = one.astype(BF16)
+            pack_q[at + 1] = two.astype(BF16)
+        for step in range(4 * quarter, 4 * quarter + 4):
             leave(0, step).start()
 
     acc_q[...] = jnp.zeros_like(acc_q)
     acc_k[...] = jnp.zeros_like(acc_k)
     acc_v[...] = jnp.zeros_like(acc_v)
-    ring_one(1, 0)
-    for group in range(4):
-        ring_one(0, group)
-        lay_queries(0, (2 * group, 2 * group + 1))
-    ring_two(1, 0)
-    for slot in range(3):
-        lay_keys(0, slot)
-    ring_end(1, 0)
-    lay_keys(0, 3)
+    ring_one(0)
+    lay(0, (0,))
+    ring_two(0)
+    lay(0, (1, 2))
+    ring_one(1)
+    ring_end(0)
+    lay(0, (3,))
 
     def before(turn):
-        quarter, slot = divmod(turn, 4)
         if turn == 1:
-            for group in range(4):
-                ring_two(0, group)
-            for place in (1, 2):
-                lay_queries(place, range(HEADS // 2))
+            ring_two(1)
+            ring_one(2)
+            lay(1, (0, 1, 2))
+            ring_end(1)
+            lay(1, (3,))
+        if turn == 2:
+            ring_two(2)
         if turn == 3:
-            for group in range(4):
-                ring_end(0, group)
-            lay_queries(3, range(HEADS // 2))
-        if slot == 0 and quarter > 0:
-            send_keys(quarter - 1)
-            ring_end(1, quarter)
-            for place in range(4):
-                lay_keys(quarter, place)
-        if slot == 1 and quarter < 3:
-            ring_one(1, quarter + 1)
-        if slot == 2 and quarter < 3:
-            ring_two(1, quarter + 1)
-        if slot == 2 and quarter > 0:
-            return_keys(quarter - 1)
-        if quarter == 3 and slot > 0:
-            send_queries(slot)
-
-    def tile(turn, carry):
-        quarter = lax.div(turn, 4)
-        slot = lax.rem(turn + lax.div(quarter, 3), 4)
-        for at in range(16):
-            if at > 0:
-                pl.when(turn == at)(lambda at=at: before(at))
-        scores = jnp.dot(qa[slot], ka[quarter], preferred_element_type=F32)
+            ring_one(3)
+        if turn == 4:
+            ring_end(2)
+            lay(2, range(4))
+        if turn == 5:
+            ring_two(3)
+        if turn == 9:
+            ring_end(3)
+            lay(3, range(4))
+        if turn == 11:
+            send_queries(0)
+        if turn == 12:
+            send_queries(1)
+        if turn == 13:
+            send_keys(3)
+            send_queries(2)
+            return_queries(0)
+        if turn == 14:
+            send_keys(1)
+            return_queries(1)
+        if turn == 15:
+            send_keys(2)
+            return_keys(3)
+            return_queries(2)
+
+    def tile(turn, codes):
+        code_q, code_k = codes
+        query, key = 3 - lax.rem(code_q, 4), lax.rem(code_k, 4)
+        for at in range(1, 16):
+            pl.when(turn == at)(lambda at=at: before(at))
+        scores = jnp.dot(qa[query], ka[key], preferred_element_type=F32)
         probs = jnp.exp2(scores * (SCALING * LOG2E))
-        grad_probs = jnp.dot(ga[slot], va[quarter], preferred_element_type=F32)
+        grad_probs = jnp.dot(ga[query], va[key], preferred_element_type=F32)
         grad_scores = (probs * grad_probs).astype(BF16)
-        acc_v[...] += jnp.dot(gt[slot], probs.astype(BF16), preferred_element_type=F32)
-        acc_k[...] += jnp.dot(qt[slot], grad_scores, preferred_element_type=F32)
-        acc_q[slot] += lax.dot_general(
-            kt[quarter], grad_scores, (((1,), (1,)), ((), ())), preferred_element_type=F32
-        )
-        return carry
-
-    lax.fori_loop(0, 16, tile, 0)
-    send_keys(3)
-    return_queries()
-    return_keys(3)
+        acc_v[key] += jnp.dot(gt[query], probs.astype(BF16), preferred_element_type=F32)
+        acc_k[key] += jnp.dot(qt[query], grad_scores, preferred_element_type=F32)
+        acc_q[query] += lax.dot_general(
+            kt[key], grad_scores, (((1,), (1,)), ((), ())), preferred_element_type=F32
+        )
+        return lax.div(code_q, 4), lax.div(code_k, 4)
+
+    lax.fori_loop(0, 16, tile, (jnp.int32(QUERY_CODE), jnp.int32(KEY_CODE)))
+    send_keys(0)
+    send_queries(3)
+    return_keys(1)
+    return_keys(2)
+    return_queries(3)
+    return_keys(0)
 
     for step in range(HEADS):
         for which in (0, 1):
@@ -316,8 +338,8 @@
             for kind in range(4):
                 ring(which, group, kind).wait_send()
     for slot in range(3):
-        sum_queries(slot).wait_send()
         for quarter in range(4):
+            sum_queries(quarter, slot).wait_send()
             sum_keys(quarter, slot).wait_send()
 
 
@@ -351,13 +373,12 @@
             low_bits(RING, PAIR, GROUP),
             low_bits(RING, DIM, GROUP),
             full(RING, DIM, GROUP),
-            full(DIM, GROUP),
-            full(DIM, GROUP),
+            full(RING, DIM, GROUP),
+            full(RING, DIM, GROUP),
             low_bits(RING, 3, 2, DIM, QUARTER),
             low_bits(RING, 3, 2, DIM, QUARTER),
-            full(RING, 2, DIM, QUARTER),
-            low_bits(3, DIM, GROUP),
-            low_bits(3, DIM, GROUP),
+            low_bits(RING, 3, DIM, QUARTER),
+            low_bits(RING, 3, DIM, QUARTER),
             low_bits(HEADS, DIM, PAIR),
             low_bits(HEADS, TOP, PAIR),
             low_bits(HEADS, DIM, PAIR),
@@ -369,8 +390,8 @@
             dma((2, 4, 4)),
             dma((4, 3)),
             dma((4, 3)),
-            dma((3,)),
-            dma((3,)),
+            dma((4, 3)),
+            dma((4, 3)),
             dma((2, HEADS)),
             dma((2, HEADS)),
         ],

time: 99.6 us -> 93.4 us (0.938)
  Pallas kernels: 95.5 us -> 89.3 us
    pallas_call x1, Pallas kernels: 95.5 us -> 89.3 us  [on_device(): pl.pallas_call(kernel, out_shape=[out] * 3, in_specs=[VMEM] * 7, out_spec...]
where the time goes in v3:
time: 93.4 us; the launch traced here: 93.3 us
  Pallas kernels  89.3 us (96%)
  local copies, waits for them, and re-layouts  3.28 us (4%)
    pallas_call x1, Pallas kernels, on_device(): pl.pallas_call(kernel, out_shape=[out] * 3, in_specs=[VMEM] * 7, out_spec...  89.3 us
    unnamed x7, local copies, waits for them, and re-layouts  3.28 us

profile of v3, /device:TPU:1, one launch (start us, length us, event | category | flops | bytes accessed | tf_op | source)
XLA Modules:
  0.0 93.3 jit_solution(5795483403364737349)
XLA Ops:
  0.6 89.3 %shard_map.94 = (bf16[64,1280]{1,0:T(8,128)(2,1)}, bf16[64,1280]{1,0:T(8,128)(2,1)}, bf16[64,1280]{1,0:T(8,128)(2,1)}) custom-call(bf16[64,1280]{1,0:T(8,128)(2,1)} %q_ref.1, bf16[64,1280]{1,0:T(8,128)(2,1)} %g_ref.1, bf16[64,1280]{1,0:T(8,128)(2,1)} %o_ref.1, bf16[64,1280]{1,0:T(8,128)(2,1)} %k_ref.1, bf16[64,1280]{1,0:T(8,128)(2,1)} %v_ref.1, ...), custom_call_target="tpu_custom_call" | custom-call | tf_op jit(solution)/shard_map/pallas_call | solution.py:356
  90.0 0.0 copy-start.1
  90.0 1.6 %copy.13 = bf16[64,1280]{1,0:T(8,128)(2,1)} copy(bf16[64,1280]{1,0:T(8,128)(2,1)} %get-tuple-element.6) | data formatting | bytes 327680
  91.6 0.0 copy-done.1
  91.6 0.0 copy-start
  91.6 0.7 copy.14
  92.3 0.3 copy-done
  92.6 0.7 copy.15
Async XLA Ops:
  90.0 1.6 %copy-start.1 = (bf16[64,1280]{1,0:T(8,128)(2,1)S(1)}, bf16[64,1280]{1,0:T(8,128)(2,1)}, u32[]{:S(2)}) copy-start(bf16[64,1280]{1,0:T(8,128)(2,1)} %get-tuple-element.7) | copy-start | bytes 491524
  91.6 1.0 %copy-start = (bf16[64,1280]{1,0:T(8,128)(2,1)S(1)}, bf16[64,1280]{1,0:T(8,128)(2,1)}, u32[]{:S(2)}) copy-start(bf16[64,1280]{1,0:T(8,128)(2,1)} %get-tuple-element.8) | copy-start | bytes 491524
